TPU v7x, 256 devices: a whole 4x4x8 slice. The times are simulated.
256 devices in a mesh: ctx: 32 (over x, z), head: 8 (over y, core).
Axes of the slice: x: 4, y: 4, z: 8, core: 2. Of those that a mesh axis runs over, the one named last changes fastest.
Arguments:
- q_clean: bfloat16 [8192, 4096], P(('ctx', 'head')), may hold values from -14 to 14, as said below
- k_clean: bfloat16 [8192, 1024], P(('ctx', 'head')), may hold values from -14 to 14, as said below
- v_clean: bfloat16 [8192, 1024], P(('ctx', 'head')), may hold values from -6 to 6
- q_noised: bfloat16 [8192, 4096], P(('ctx', 'head')), may hold values from -14 to 14, as said below
- masked: int32 [8192], P('ctx'), may hold values 0 or 1
- noise_level: int32 [256], P('ctx'), may hold values from 0 to 7
- mask_key: bfloat16 [8, 1024], P(None, 'head'), may hold values from -6 to 6
- mask_value: bfloat16 [8, 1024], P(None, 'head'), may hold values from -6 to 6
- d_clean: bfloat16 [8192, 4096], P(('ctx', 'head')), may hold values from -6 to 6
- d_noised: bfloat16 [8192, 4096], P(('ctx', 'head')), may hold values from -6 to 6
Outputs:
- out_clean: bfloat16 [8192, 4096], P(('ctx', 'head'))
- out_noised: bfloat16 [8192, 4096], P(('ctx', 'head'))
- dq_clean: bfloat16 [8192, 4096], P(('ctx', 'head'))
- dq_noised: bfloat16 [8192, 4096], P(('ctx', 'head'))
- dk_clean: bfloat16 [8192, 1024], P(('ctx', 'head'))
- dv_clean: bfloat16 [8192, 1024], P(('ctx', 'head'))
Inputs may be any that keep to these rules, and one draw needn't show every extreme that they name: `q_clean`: bounded entries. `k_clean`: bounded entries. `q_noised`: bounded entries.
All inputs are finite; a program needn't handle non-finite values. No bound on the sum of `masked` on one device may be relied on, other than what follows from the above.
Results may differ from a plain program's by a relative error of at most 0.029.
Values may be sent and summed in bfloat16 or wider, within the bound.
No kernel may reach another device: no remote copies, remote signals or barrier semaphores. Data moves between devices by JAX's collectives and lax.ppermute only.
A program may use at most 128 MiB of HBM per device.

v0:
```python
import math

import jax
import jax.numpy as jnp
from jax import lax
from jax.sharding import PartitionSpec as P

HD = 128
BLOCK = 32
LEVELS = 8


big_negative = -1e30


def block_width(total_rows):
    return math.gcd(total_rows, 512)


def kept_clean(begin_at, span_width, limits):
    key_block = (begin_at + jnp.arange(span_width, dtype=jnp.int32)) // BLOCK
    return key_block[None, :] <= limits[:, None]


def attend_step(carried, queries, key_rows, value_rows, visible):
    running_max, running_sum, weighted = carried
    scaling = 1.0 / math.sqrt(HD)
    scores = (
        jnp.einsum("tkgd,skd->kgts", queries, key_rows, preferred_element_type=jnp.float32)
        * scaling
    )
    scores = jnp.where(visible, scores, big_negative)
    new_max = jnp.maximum(running_max, jnp.max(scores, axis=-1))
    weights = jnp.where(visible, jnp.exp(scores - new_max[..., None]), 0.0)
    factor = jnp.exp(running_max - new_max)
    running_sum = running_sum * factor + jnp.sum(weights, axis=-1)
    weighted = weighted * factor[..., None] + jnp.einsum(
        "kgts,skd->kgtd",
        weights.astype(jnp.bfloat16),
        value_rows,
        preferred_element_type=jnp.float32,
    )
    return (new_max, running_sum, weighted)


def fold_clean(carried, queries, key_rows, value_rows, first_key, limits):
    total_rows = key_rows.shape[0]
    span_width = block_width(total_rows)
    block_count = total_rows // span_width
    kv_heads = key_rows.shape[1] // HD
    key_blocks = key_rows.reshape(block_count, span_width, kv_heads, HD)
    value_blocks = value_rows.reshape(block_count, span_width, kv_heads, HD)
    starts = first_key + span_width * jnp.arange(block_count, dtype=jnp.int32)
    top_limit = jnp.max(limits)

    def fold_advance(state_now, element):
        key_part, value_part, begin_at = element

        def fold_run(state_in):
            return attend_step(
                state_in, queries, key_part, value_part, kept_clean(begin_at, span_width, limits)
            )

        def keep(state_in):
            return state_in

        return (lax.cond(begin_at // BLOCK <= top_limit, fold_run, keep, state_now), None)

    carried, _ = lax.scan(fold_advance, carried, (key_blocks, value_blocks, starts))
    return carried


def grad_step(queries, grad_rows, log_total, row_terms, key_rows, value_rows, visible):
    scaling = 1.0 / math.sqrt(HD)
    scores = (
        jnp.einsum("tkgd,skd->kgts", queries, key_rows, preferred_element_type=jnp.float32)
        * scaling
    )
    weights = jnp.where(
        visible, jnp.exp(jnp.where(visible, scores, big_negative) - log_total[..., None]), 0.0
    )
    rounded = weights.astype(jnp.bfloat16)
    weight_grads = jnp.einsum(
        "tkgd,skd->kgts", grad_rows, value_rows, preferred_element_type=jnp.float32
    )
    score_grads = (weights * (weight_grads - row_terms[..., None]) * scaling).astype(jnp.bfloat16)
    return (rounded, score_grads)


def key_terms(queries, grad_rows, rounded, score_grads):
    key_part = jnp.einsum(
        "kgts,tkgd->skd", score_grads, queries, preferred_element_type=jnp.float32
    )
    value_part = jnp.einsum(
        "kgts,tkgd->skd", rounded, grad_rows, preferred_element_type=jnp.float32
    )
    span_width = key_part.shape[0]
    return jnp.concatenate(
        [key_part.reshape(span_width, -1), value_part.reshape(span_width, -1)], axis=1
    )


def grad_span(queries, grad_rows, log_total, row_terms, key_rows, value_rows, first_key, limits):
    total_rows = key_rows.shape[0]
    span_width = block_width(total_rows)
    block_count = total_rows // span_width
    kv_heads = key_rows.shape[1] // HD
    key_blocks = key_rows.reshape(block_count, span_width, kv_heads, HD)
    value_blocks = value_rows.reshape(block_count, span_width, kv_heads, HD)
    starts = first_key + span_width * jnp.arange(block_count, dtype=jnp.int32)
    query_grads = jnp.zeros(queries.shape, jnp.float32)
    top_limit = jnp.max(limits)

    def grad_advance(summed, element):
        key_part, value_part, begin_at = element

        def grad_run(summed_in):
            rounded, score_grads = grad_step(
                queries,
                grad_rows,
                log_total,
                row_terms,
                key_part,
                value_part,
                kept_clean(begin_at, span_width, limits),
            )
            summed_in = summed_in + jnp.einsum(
                "kgts,skd->tkgd", score_grads, key_part, preferred_element_type=jnp.float32
            )
            result = None
            result = key_terms(queries, grad_rows, rounded, score_grads)
            return (summed_in, result)

        def skip(summed_in):
            result = None
            result = jnp.zeros((span_width, 2 * kv_heads * HD), jnp.float32)
            return (summed_in, result)

        return lax.cond(begin_at // BLOCK <= top_limit, grad_run, skip, summed)

    query_grads, stacked = lax.scan(grad_advance, query_grads, (key_blocks, value_blocks, starts))
    stacked = stacked.reshape(total_rows, -1)
    return (query_grads, stacked)


def on_device(
    q_clean,
    k_clean,
    v_clean,
    q_noised,
    masked,
    noise_level,
    mask_key,
    mask_value,
    d_clean,
    d_noised,
):
    moved = (
        lax.all_to_all(q_clean, "head", split_axis=1, concat_axis=0, tiled=True),
        lax.all_to_all(q_noised, "head", split_axis=1, concat_axis=0, tiled=True),
        lax.all_to_all(k_clean, "head", split_axis=1, concat_axis=0, tiled=True),
        lax.all_to_all(v_clean, "head", split_axis=1, concat_axis=0, tiled=True),
        lax.all_to_all(d_clean, "head", split_axis=1, concat_axis=0, tiled=True),
        lax.all_to_all(d_noised, "head", split_axis=1, concat_axis=0, tiled=True),
    )
    query_clean, query_noised, key_here, value_here, grad_clean, grad_noised = moved
    row_count = query_clean.shape[0]
    kv_heads = key_here.shape[1] // HD
    group_size = query_clean.shape[1] // key_here.shape[1]
    kv_cols = kv_heads * HD
    first_row = lax.axis_index("ctx") * row_count
    query_block = (first_row + jnp.arange(row_count, dtype=jnp.int32)) // BLOCK
    limits = jnp.concatenate([query_block, query_block - 1])
    row_blocks = jnp.concatenate([query_block, query_block])
    noised_row = jnp.arange(2 * row_count, dtype=jnp.int32) >= row_count
    kept_self = (row_blocks[:, None] == query_block[None, :]) & noised_row[:, None]
    levels_onehot = (noise_level[:, None] == jnp.arange(LEVELS, dtype=jnp.int32)[None, :]).astype(
        jnp.bfloat16
    )
    table_rows = jnp.dot(
        levels_onehot,
        jnp.concatenate([mask_key, mask_value], axis=1),
        preferred_element_type=jnp.float32,
    ).astype(jnp.bfloat16)
    table_rows = jnp.repeat(table_rows, BLOCK, axis=0)
    covered = masked[:, None] == 1
    noised_keys = jnp.where(covered, table_rows[:, :kv_cols], key_here).reshape(
        row_count, kv_heads, HD
    )
    noised_values = jnp.where(covered, table_rows[:, kv_cols:], value_here).reshape(
        row_count, kv_heads, HD
    )
    queries = jnp.concatenate([query_clean, query_noised], axis=0).reshape(
        2 * row_count, kv_heads, group_size, HD
    )
    grad_rows = jnp.concatenate([grad_clean, grad_noised], axis=0).reshape(
        2 * row_count, kv_heads, group_size, HD
    )
    carried = (
        jnp.full((kv_heads, group_size, 2 * row_count), big_negative, jnp.float32),
        jnp.zeros((kv_heads, group_size, 2 * row_count), jnp.float32),
        jnp.zeros((kv_heads, group_size, 2 * row_count, HD), jnp.float32),
    )
    carried = attend_step(carried, queries, noised_keys, noised_values, kept_self)
    clean_keys, clean_values = (
        lax.all_gather(key_here, "ctx", axis=0, tiled=True),
        lax.all_gather(value_here, "ctx", axis=0, tiled=True),
    )
    carried = fold_clean(carried, queries, clean_keys, clean_values, 0, limits)
    running_max, running_sum, weighted = carried
    attended = weighted / running_sum[..., None]
    log_total = running_max + jnp.log(running_sum)
    attended_rows = jnp.transpose(attended, (2, 0, 1, 3))
    row_terms = jnp.transpose(
        jnp.sum(grad_rows.astype(jnp.float32) * attended_rows, axis=-1), (1, 2, 0)
    )
    rounded, score_grads = grad_step(
        queries, grad_rows, log_total, row_terms, noised_keys, noised_values, kept_self
    )
    query_grads = jnp.einsum(
        "kgts,skd->tkgd", score_grads, noised_keys, preferred_element_type=jnp.float32
    )
    self_terms = key_terms(queries, grad_rows, rounded, score_grads)
    self_terms = jnp.where((masked == 0)[:, None], self_terms, 0.0)
    clean_part, stacked = grad_span(
        queries, grad_rows, log_total, row_terms, clean_keys, clean_values, 0, limits
    )
    query_grads = query_grads + clean_part
    shares = lax.psum_scatter(
        stacked.astype(jnp.bfloat16), "ctx", scatter_dimension=0, tiled=True
    ).astype(jnp.float32)
    shares = shares + self_terms
    key_grads = shares[:, :kv_cols].astype(jnp.bfloat16)
    value_grads = shares[:, kv_cols:].astype(jnp.bfloat16)
    out_rows = attended_rows.reshape(2 * row_count, -1).astype(jnp.bfloat16)
    query_rows = query_grads.reshape(2 * row_count, -1).astype(jnp.bfloat16)
    returned = (
        lax.all_to_all(out_rows[:row_count], "head", split_axis=0, concat_axis=1, tiled=True),
        lax.all_to_all(out_rows[row_count:], "head", split_axis=0, concat_axis=1, tiled=True),
        lax.all_to_all(query_rows[:row_count], "head", split_axis=0, concat_axis=1, tiled=True),
        lax.all_to_all(query_rows[row_count:], "head", split_axis=0, concat_axis=1, tiled=True),
        lax.all_to_all(key_grads, "head", split_axis=0, concat_axis=1, tiled=True),
        lax.all_to_all(value_grads, "head", split_axis=0, concat_axis=1, tiled=True),
    )
    return (returned[0], returned[1], returned[2], returned[3], returned[4], returned[5])


def solution(mesh):
    return jax.shard_map(
        on_device,
        mesh=mesh,
        in_specs=(
            P(("ctx", "head"), None),
            P(("ctx", "head"), None),
            P(("ctx", "head"), None),
            P(("ctx", "head"), None),
            P("ctx"),
            P("ctx"),
            P(None, "head"),
            P(None, "head"),
            P(("ctx", "head"), None),
            P(("ctx", "head"), None),
        ),
        out_specs=(
            P(("ctx", "head"), None),
            P(("ctx", "head"), None),
            P(("ctx", "head"), None),
            P(("ctx", "head"), None),
            P(("ctx", "head"), None),
            P(("ctx", "head"), None),
        ),
        check_vma=False,
    )
```

profile of v0, /device:TPU:1, one launch (start us, length us, event | category | flops | bytes accessed | tf_op | source)
XLA Modules:
  0.0 795.0 jit_solution(12043759146517557383)
XLA Ops:
  7.3 0.8 copy-done
  8.0 11.1 %all_to_all.216 = bf16[32,8,128]{2,0,1:T(8,128)(2,1)} all-to-all(bf16[32,8,128]{2,0,1:T(8,128)(2,1)S(1)} %copy_bitcast_fusion.7), channel_id=1, replica_groups=mesh['ctx'=32,'head'=8] {'head'}, dimensions={1} | all-to-all | bytes 131072 | tf_op jit(solution)/shard_map/all_to_all | solution.py:161
  19.2 0.9 copy_bitcast_fusion.6
  20.1 8.7 %all_to_all.217 = bf16[32,8,128]{2,0,1:T(8,128)(2,1)} all-to-all(bf16[32,8,128]{2,0,1:T(8,128)(2,1)S(1)} %copy_bitcast_fusion.6), channel_id=1, replica_groups=mesh['ctx'=32,'head'=8] {'head'}, dimensions={1} | all-to-all | bytes 131072 | tf_op jit(solution)/shard_map/all_to_all | solution.py:162
  28.8 1.7 copy.209
  30.5 4.1 all-to-all-start.1
  34.6 1.7 copy.208
  36.3 4.8 all-to-all-done.1
  41.1 4.4 all-to-all-start.2
  45.5 1.7 copy.207
  47.1 1.3 broadcast_compare_fusion.2
  48.4 3.5 all-to-all-done.2
  52.0 4.4 all-to-all-start.6
  56.3 1.7 copy.206
  58.2 4.6 all-to-all-done.6
  62.9 4.4 all-to-all-start.7
  69.6 4.2 all-to-all-done.7
  74.0 1.0 copy.151
  76.4 0.9 copy-done.1
  77.3 0.8 fusion.82
  78.1 15.8 %all-gather.3.cloned.1.call-done = bf16[8192,128]{1,0:T(8,128)(2,1)} async-done(((bf16[256,128]{1,0:T(8,128)(2,1)}), bf16[8192,128]{1,0:T(8,128)(2,1)}) %all-gather.3.cloned.1.call-update) | async-done | bytes 2097168 | tf_op jit(solution)/shard_map/all_gather | solution.py:206
  93.9 77.7 %all-gather.5.cloned.1.call-done = bf16[8192,128]{1,0:T(8,128)(2,1)} async-done(((bf16[256,128]{1,0:T(8,128)(2,1)}), bf16[8192,128]{1,0:T(8,128)(2,1)}) %all-gather.5.cloned.1.call-update) | async-done | bytes 2097168 | tf_op jit(solution)/shard_map/all_gather | solution.py:207
  171.7 58.3 %while.33 = (s32[]{:T(128)}, f32[1,4,512]{2,1,0:T(4,128)S(1)}, f32[1,4,512]{2,1,0:T(4,128)S(1)}, f32[1,4,512,128]{3,2,1,0:T(8,128)S(1)}, s32[16]{0:T(128)S(1)}, ...) while((s32[]{:T(128)}, f32[1,4,512]{2,1,0:T(4,128)S(1)}, ...), condition=%wide.region_9.10_spmd, body=%wide.region_4.9_spmd.sunk | while | flops 551303168 | bytes 16653769 | solution.py:69
  174.9 6.6 conditional.4
  175.8 1.8 fusion
  177.6 2.8 fusion.10
  180.4 1.0 fusion.2
  230.6 1.2 fusion.89
  232.0 72.9 %while.34 = (s32[]{:T(128)}, f32[512,1,4,128]{0,3,2,1:T(8,128)S(1)}, bf16[16,512,256]{1,2,0:T(8,128)(2,1)}, s32[16]{0:T(128)S(1)}, s32[]{:T(128)}, /*index=5*/bf...) while((s32[]{:T(128)}, ...), condition=%wide.region_14.15_spmd, body=%wide.region_11.14_spmd.sunk | while | flops 1356865536 | bytes 27755020 | solution.py:141
  235.2 9.1 %conditional.5 = (f32[512,1,4,128]{0,3,2,1:T(8,128)S(1)}, bf16[1,512,256]{1,2,0:T(8,128)(2,1)S(1)}) conditional(s32[]{:T(128)} %convert_element_type.115, f32[512,1,4,128]{0,3,2,1:T(8,128)S(1)} %get-tuple-element.828, (bf16[16,512,1,128]{3,1,2,0:T(8,128)(2,1)}, s32[]{:T(128)}, s32[]{:T(128)}, s32[512]{0:T(512)S(1)}, ...), branch_computations={%region_12.12_spmd, %region_13.13_spmd} | conditional | flops 1356865536 | bytes 27229800 | solution.py:139
  236.2 1.6 fusion.58
  237.8 2.7 fusion.30
  240.6 1.6 fusion.49
  242.1 1.4 fusion.46
  243.5 0.8 fusion.52
  264.3 0.7 constant_dynamic-update-slice_fusion.2
  280.2 0.7 constant_dynamic-update-slice_fusion.2
  284.2 0.7 constant_dynamic-update-slice_fusion.2
  288.2 0.7 constant_dynamic-update-slice_fusion.2
  292.2 0.7 constant_dynamic-update-slice_fusion.2
  304.9 4.8 copy.191
  310.4 0.8 all_to_all.178
  311.2 8.8 %all-to-all-start.5 = ((bf16[8,32,512]{2,1,0:T(8,128)(2,1)}), bf16[8,32,512]{2,1,0:T(8,128)(2,1)}, u32[]{:S(2)}, u32[]{:S(2)}) async-start(bf16[8,32,512]{2,1,0:T(8,128)(2,1)} %all_to_all.178), calls=%async_computation.5 | async-start | bytes 524288 | tf_op jit(solution)/shard_map/all_to_all | solution.py:239
  320.2 0.8 all_to_all.174
  321.0 2.4 fusion.81
  323.5 1.2 fusion.84
  324.7 1.9 all-to-all-done.5
  326.6 4.4 all-to-all-start.4
  331.0 1.1 fusion.118
  332.2 0.8 all_to_all.192
  333.2 0.8 all_to_all.188
  334.5 3.0 all-to-all-done.4
  337.5 4.4 all-to-all-start.9
  341.9 2.1 convolution_bitcast_fusion.1
  344.0 4.4 all-to-all-done.9
  348.4 4.4 all-to-all-start.8
  352.7 409.0 %reduce-scatter.2.cloned.1.call-done = bf16[256,256]{0,1:T(8,128)(2,1)} async-done(((bf16[8192,256]{0,1:T(8,128)(2,1)}), bf16[256,256]{0,1:T(8,128)(2,1)}) %reduce-scatter.2.cloned.1.call-update) | async-done | bytes 131088 | tf_op jit(solution)/shard_map/reduce_scatter | solution.py:229
  761.8 0.9 fusion.101
  762.7 0.7 copy.163
  763.5 10.1 %all-to-all-start.11 = ((bf16[8,32,128]{2,1,0:T(8,128)(2,1)}), bf16[8,32,128]{2,1,0:T(8,128)(2,1)S(1)}, u32[]{:S(2)}, u32[]{:S(2)}) async-start(bf16[8,32,128]{2,1,0:T(8,128)(2,1)} %bitcast.90), calls=%async_computation.12 | async-start | bytes 131072 | tf_op jit(solution)/shard_map/all_to_all | solution.py:243
  773.6 1.7 copy.188
  777.4 0.7 copy.161
  778.4 4.5 all-to-all-start.10
  783.6 4.2 all-to-all-done.10
  (183 shorter events, 39.8 us)
Async XLA Ops:
  7.2 0.8 copy-start
  7.2 50.8 %copy-start.18 = (bf16[8,128]{1,0:T(8,128)(2,1)S(1)}, bf16[8,128]{1,0:T(8,128)(2,1)}, u32[]{:S(2)}) copy-start(bf16[8,128]{1,0:T(8,128)(2,1)} %param.25) | copy-start | bytes 6148
  7.2 50.8 %copy-start.19 = (bf16[8,128]{1,0:T(8,128)(2,1)S(1)}, bf16[8,128]{1,0:T(8,128)(2,1)}, u32[]{:S(2)}) copy-start(bf16[8,128]{1,0:T(8,128)(2,1)} %param.24) | copy-start | bytes 6148
  7.2 50.8 %copy-start.20 = (s32[8]{0:T(128)S(1)}, s32[8]{0:T(128)}, u32[]{:S(2)}) copy-start(s32[8]{0:T(128)} %param.23) | copy-start | bytes 100
  7.2 86.7 %all-gather.3.cloned.1.call-start = ((), (), s32[]{:S(2)}) async-start(), calls=%async_computation.13 | async-start | bytes 2162688 | tf_op jit(solution)/shard_map/all_gather | solution.py:206
  19.2 152.5 %all-gather.5.cloned.1.call-start = ((), (), s32[]{:S(2)}) async-start(), calls=%async_computation.14 | async-start | bytes 2162688 | tf_op jit(solution)/shard_map/all_gather | solution.py:207
  30.5 10.6 %all-to-all-start.1 = ((bf16[32,8,512]{2,0,1:T(8,128)(2,1)}), bf16[32,8,512]{2,0,1:T(8,128)(2,1)S(1)}, u32[]{:S(2)}, u32[]{:S(2)}) async-start(bf16[32,8,512]{2,0,1:T(8,128)(2,1)} %bitcast.311), calls=%async_computation.1 | async-start | bytes 524288 | tf_op jit(solution)/shard_map/all_to_all | solution.py:159
  41.1 10.9 %all-to-all-start.2 = ((bf16[32,8,512]{2,0,1:T(8,128)(2,1)}), bf16[32,8,512]{2,0,1:T(8,128)(2,1)S(1)}, u32[]{:S(2)}, u32[]{:S(2)}) async-start(bf16[32,8,512]{2,0,1:T(8,128)(2,1)} %bitcast.310), calls=%async_computation.2 | async-start | bytes 524288 | tf_op jit(solution)/shard_map/all_to_all | solution.py:160
  47.1 28.2 %copy-start.6 = (bf16[32,8,128]{2,0,1:T(8,128)(2,1)S(1)}, bf16[32,8,128]{2,0,1:T(8,128)(2,1)}, u32[]{:S(2)}) copy-start(bf16[32,8,128]{2,0,1:T(8,128)(2,1)} %all_to_all.216) | copy-start | bytes 196612
  48.4 28.0 %copy-start.13 = (pred[256]{0:T(512)(128)(4,1)}, pred[256]{0:T(512)(128)(4,1)S(1)}, u32[]{:S(2)}) copy-start(pred[256]{0:T(512)(128)(4,1)S(1)} %get-tuple-element.604) | copy-start | bytes 772
  52.0 10.9 %all-to-all-start.6 = ((bf16[32,8,512]{2,0,1:T(8,128)(2,1)}), bf16[32,8,512]{2,0,1:T(8,128)(2,1)S(1)}, u32[]{:S(2)}, u32[]{:S(2)}) async-start(bf16[32,8,512]{2,0,1:T(8,128)(2,1)} %bitcast.309), calls=%async_computation.6 | async-start | bytes 524288 | tf_op jit(solution)/shard_map/all_to_all | solution.py:163
  62.9 10.9 %all-to-all-start.7 = ((bf16[32,8,512]{2,0,1:T(8,128)(2,1)}), bf16[32,8,512]{2,0,1:T(8,128)(2,1)S(1)}, u32[]{:S(2)}, u32[]{:S(2)}) async-start(bf16[32,8,512]{2,0,1:T(8,128)(2,1)} %bitcast.308), calls=%async_computation.7 | async-start | bytes 524288 | tf_op jit(solution)/shard_map/all_to_all | solution.py:164
  67.2 694.6 %reduce-scatter.2.cloned.1.call-start = ((), (), s32[]{:S(2)}) async-start(), calls=%async_computation.15 | async-start | bytes 4325376 | tf_op jit(solution)/shard_map/reduce_scatter | solution.py:229
  69.3 7.1 copy-start.4
  74.0 156.7 %copy-start.2 = (bf16[512,1,4,128]{3,0,2,1:T(8,128)(2,1)}, bf16[512,1,4,128]{3,0,2,1:T(8,128)(2,1)S(1)}, u32[]{:S(2)}) copy-start(bf16[512,1,4,128]{3,0,2,1:T(8,128)(2,1)S(1)} %copy_dynamic-update-slice_fusion) | copy-start | bytes 1572868
  74.0 3.3 copy-start.9
  75.3 2.7 copy-start.7
  76.0 1.4 copy-start.1
  235.2 2.6 copy-start.10
  235.2 2.6 copy-start.11
  235.3 2.6 copy-start.15
  309.7 11.3 %copy-start.3 = (bf16[512,1,4,128]{3,0,2,1:T(8,128)(2,1)S(1)}, bf16[512,1,4,128]{3,0,2,1:T(8,128)(2,1)}, u32[]{:S(2)}) copy-start(bf16[512,1,4,128]{3,0,2,1:T(8,128)(2,1)} %copy-done.2) | copy-start | bytes 1572868
  309.7 11.3 %copy-start.5 = (pred[512,256]{0,1:T(8,128)(4,1)S(1)}, pred[512,256]{0,1:T(8,128)(4,1)}, u32[]{:S(2)}) copy-start(pred[512,256]{0,1:T(8,128)(4,1)} %copy-done.4) | copy-start | bytes 393220
  309.7 11.3 %copy-start.8 = (bf16[8,32,256]{2,1,0:T(8,128)(2,1)S(1)}, bf16[8,32,256]{2,1,0:T(8,128)(2,1)}, u32[]{:S(2)}) copy-start(bf16[8,32,256]{2,1,0:T(8,128)(2,1)} %copy-done.7) | copy-start | bytes 393220
  309.7 11.3 %copy-start.12 = (f32[1,4,512]{2,1,0:T(4,128)S(1)}, f32[1,4,512]{2,1,0:T(4,128)}, u32[]{:S(2)}) copy-start(f32[1,4,512]{2,1,0:T(4,128)} %get-tuple-element.890) | copy-start | bytes 24580
  310.1 13.4 %copy-start.14 = (pred[256]{0:T(512)(128)(4,1)S(1)}, pred[256]{0:T(512)(128)(4,1)}, u32[]{:S(2)}) copy-start(pred[256]{0:T(512)(128)(4,1)} %copy-done.13) | copy-start | bytes 772
  311.2 15.5 %all-to-all-start.5 = ((bf16[8,32,512]{2,1,0:T(8,128)(2,1)}), bf16[8,32,512]{2,1,0:T(8,128)(2,1)}, u32[]{:S(2)}, u32[]{:S(2)}) async-start(bf16[8,32,512]{2,1,0:T(8,128)(2,1)} %all_to_all.178), calls=%async_computation.5 | async-start | bytes 524288 | tf_op jit(solution)/shard_map/all_to_all | solution.py:239
  323.5 18.4 %copy-start.16 = (f32[1,4,512]{2,1,0:T(4,128)S(1)}, f32[1,4,512]{2,1,0:T(4,128)}, u32[]{:S(2)}) copy-start(f32[1,4,512]{2,1,0:T(4,128)} %get-tuple-element.891) | copy-start | bytes 24580
  326.6 10.9 %all-to-all-start.4 = ((bf16[8,32,512]{2,1,0:T(8,128)(2,1)}), bf16[8,32,512]{2,1,0:T(8,128)(2,1)S(1)}, u32[]{:S(2)}, u32[]{:S(2)}) async-start(bf16[8,32,512]{2,1,0:T(8,128)(2,1)} %all_to_all.174), calls=%async_computation.4 | async-start | bytes 524288 | tf_op jit(solution)/shard_map/all_to_all | solution.py:238
  332.0 429.7 %copy-start.17 = (pred[256]{0:T(512)(128)(4,1)S(1)}, pred[256]{0:T(512)(128)(4,1)}, u32[]{:S(2)}) copy-start(pred[256]{0:T(512)(128)(4,1)} %get-tuple-element.603) | copy-start | bytes 772
  337.5 10.9 %all-to-all-start.9 = ((bf16[8,32,512]{2,1,0:T(8,128)(2,1)}), bf16[8,32,512]{2,1,0:T(8,128)(2,1)S(1)}, u32[]{:S(2)}, u32[]{:S(2)}) async-start(bf16[8,32,512]{2,1,0:T(8,128)(2,1)} %all_to_all.192), calls=%async_computation.9 | async-start | bytes 524288 | tf_op jit(solution)/shard_map/all_to_all | solution.py:241
  348.4 415.1 %all-to-all-start.8 = ((bf16[8,32,512]{2,1,0:T(8,128)(2,1)}), bf16[8,32,512]{2,1,0:T(8,128)(2,1)S(1)}, u32[]{:S(2)}, u32[]{:S(2)}) async-start(bf16[8,32,512]{2,1,0:T(8,128)(2,1)} %all_to_all.188), calls=%async_computation.8 | async-start | bytes 524288 | tf_op jit(solution)/shard_map/all_to_all | solution.py:240
  763.5 15.0 %all-to-all-start.11 = ((bf16[8,32,128]{2,1,0:T(8,128)(2,1)}), bf16[8,32,128]{2,1,0:T(8,128)(2,1)S(1)}, u32[]{:S(2)}, u32[]{:S(2)}) async-start(bf16[8,32,128]{2,1,0:T(8,128)(2,1)} %bitcast.90), calls=%async_computation.12 | async-start | bytes 131072 | tf_op jit(solution)/shard_map/all_to_all | solution.py:243
  778.4 9.4 %all-to-all-start.10 = ((bf16[8,32,128]{2,1,0:T(8,128)(2,1)}), bf16[8,32,128]{2,1,0:T(8,128)(2,1)S(1)}, u32[]{:S(2)}, u32[]{:S(2)}) async-start(bf16[8,32,128]{2,1,0:T(8,128)(2,1)} %bitcast.88), calls=%async_computation.11 | async-start | bytes 131072 | tf_op jit(solution)/shard_map/all_to_all | solution.py:242
Sparse Core Ops, SparseCore 0:
  19.3 74.5 all-gather.2
  96.5 75.1 all-gather.4
  309.9 451.8 reduce-scatter.1
where the time goes:
time: 800 us; the launch traced here: 795 us
  waiting for transfers between devices  534 us (67%)
  loops' own time  84 us (10%)
  local copies, waits for them, and re-layouts  59.3 us (7%)
  starting transfers between devices  53.8 us (7%)
  matrix products  20.4 us (3%)
  blocking collectives  19.8 us (2%)
  between operations  15.4 us (2%)
  other arithmetic  8.57 us (1%)
    reduce_scatter x1, waiting for transfers between devices, on_device(): lax.psum_scatter(stacked.astype(jnp.bfloat16), 'ctx', scatter_dimension=0...  409 us
    all_gather x1, waiting for transfers between devices, on_device(): lax.all_gather(value_here, 'ctx', axis=0, tiled=True)  77.7 us
    another operation x1, loops' own time, fold_clean(): lax.scan(fold_advance, carried, (key_blocks, value_blocks, starts))  42.1 us
    another operation x1, loops' own time, grad_span(): lax.scan(grad_advance, query_grads, (key_blocks, value_blocks, starts))  41.1 us
    dynamic_slice x32, local copies, waits for them, and re-layouts, fold_clean(): lax.scan(fold_advance, carried, (key_blocks, value_blocks, starts))  19.7 us
  transfers between devices with their start and end apart: 13, of which 12 were waited for; matrix products, arithmetic and copies ran while one was open for 4% of the time, Pallas kernels for 0%

commit v1 on v0

v1 whole, which is shorter than its diff:
```python
import functools
import math

import jax
import jax.numpy as jnp
from jax import lax
from jax.experimental import pallas as pl
from jax.experimental.pallas import tpu as pltpu
from jax.sharding import PartitionSpec as P
bf=jnp.bfloat16; f32=jnp.float32
HD=128; BLOCK=32; T=256; C=256; G=4
NEG=-1e30
SC=1.0/math.sqrt(HD); C2=math.log2(math.e)*SC

def dot(a,b): return jnp.dot(a,b,preferred_element_type=f32)

def kernel(c_ref, qd_ref, kv_ref, nkv_ref, keep_ref, o_ref, dkv_ref, qt, dot_t, ot, dqt, ml, *, TT, CC):
    c=c_ref[0]
    nt=2048//T
    for t in range(nt):
        q=qd_ref[:, t*128:(t+1)*128].astype(f32)
        d=qd_ref[:, 1024+t*128:1024+(t+1)*128].astype(f32)
        qs=q.T*C2
        hi=qs.astype(bf)
        qt[0:128, t*T:(t+1)*T]=hi
        qt[128:256, t*T:(t+1)*T]=(qs-hi.astype(f32)).astype(bf)
        dot_t[0:128, t*T:(t+1)*T]=d.T.astype(bf)
    kb=lax.broadcasted_iota(jnp.int32,(C,T),0)//BLOCK
    qb=lax.broadcasted_iota(jnp.int32,(C,T),1)//BLOCK
    def first(kk, vt, t, mask):
        s=jnp.where(mask, dot(kk, qt[:, t*T:(t+1)*T]), NEG)
        m=jnp.max(s,axis=0,keepdims=True)
        p=jnp.exp2(s-m)
        ml[0:1, t*T:(t+1)*T]=m
        ml[1:2, t*T:(t+1)*T]=jnp.sum(p,axis=0,keepdims=True)
        ot[:, t*T:(t+1)*T]=dot(vt,p.astype(bf))
    def step(kk, vt, lo, width, mask=None):
        sl=slice(lo,lo+width)
        s=dot(kk, qt[:, sl])
        if mask is not None: s=jnp.where(mask,s,NEG)
        mo=ml[0:1, sl]
        m=jnp.maximum(mo,jnp.max(s,axis=0,keepdims=True))
        p=jnp.exp2(s-m)
        a=jnp.exp2(mo-m)
        ml[0:1, sl]=m
        ml[1:2, sl]=ml[1:2, sl]*a+jnp.sum(p,axis=0,keepdims=True)
        ot[:, sl]=ot[:, sl]*a+dot(vt,p.astype(bf))
    own=pl.ds(pl.multiple_of(c*C,C),C)
    k_own=kv_ref[own,0:128]; v_own=kv_ref[own,128:256]
    kk=jnp.concatenate([k_own,k_own],axis=1)
    vt=v_own.astype(f32).T.astype(bf)
    nk=nkv_ref[:,0:128]; nv=nkv_ref[:,128:256]
    nkk=jnp.concatenate([nk,nk],axis=1); nvt=nv.astype(f32).T.astype(bf)
    for t in range(nt//2):
        first(kk,vt,t,kb<=qb)
    for t in range(nt//2,nt):
        first(nkk,nvt,t,kb==qb)
    for t in range(nt//2,nt):
        step(kk,vt,t*T,T,kb<qb)
    def body(j,_):
        sl=pl.ds(pl.multiple_of(j*CC,CC),CC)
        k=kv_ref[sl,0:128]; v=kv_ref[sl,128:256]
        kk=jnp.concatenate([k,k],axis=1); vt=v.astype(f32).T.astype(bf)
        for t in range(2048//TT):
            step(kk,vt,t*TT,TT)
        return 0
    nfull=c*(C//CC) if CC<=C else c
    lax.fori_loop(0,nfull,body,0)
    l=ml[1:2,:]
    ml[0:1,:]=ml[0:1,:]+jnp.log2(l)
    rl=1.0/l
    dot_t[128:256,:]=jnp.zeros((128,2048),bf)
    for t in range(nt):
        sl=slice(t*T,(t+1)*T)
        o=ot[:,sl]*rl[:,sl]
        D=-jnp.sum(o*dot_t[0:128,sl].astype(f32),axis=0,keepdims=True)
        hi=D.astype(bf).astype(f32); r=D-hi
        mid=r.astype(bf).astype(f32); lo=r-mid
        row=lax.broadcasted_iota(jnp.int32,(16,T),0)
        blk=jnp.where(row==0,hi,jnp.where(row==1,mid,jnp.where(row==2,lo,0.0)))
        dot_t[128:144,sl]=blk.astype(bf)
        o_ref[:, t*128:(t+1)*128]=o.T.astype(bf)
    dqt[...]=jnp.zeros_like(dqt)
    ones=jnp.ones((C,128),bf)
    def grads(kk,kt,va,lo,width,mask=None):
        sl=slice(lo,lo+width)
        s=dot(kk,qt[:,sl])
        if mask is not None: s=jnp.where(mask,s,NEG)
        p=jnp.exp2(s-ml[0:1,sl])
        dp=dot(va,dot_t[:,sl])
        ds=(p*dp).astype(bf)
        pb=p.astype(bf)
        dqt[:,sl]=dqt[:,sl]+dot(kt,ds)
        tiles=range(lo//T,(lo+width)//T)
        qr=jnp.concatenate([qd_ref[:, t*128:(t+1)*128] for t in tiles],axis=0)
        dr=jnp.concatenate([qd_ref[:, 1024+t*128:1024+(t+1)*128] for t in tiles],axis=0)
        return dot(ds,qr), dot(pb,dr)
    def prep(k,v):
        n=k.shape[0]
        return jnp.concatenate([k,k],axis=1), k.astype(f32).T.astype(bf), jnp.concatenate([v,jnp.ones((n,128),bf)],axis=1)
    kk,kt,va=prep(k_own,v_own)
    dk=jnp.zeros((C,128),f32); dv=jnp.zeros((C,128),f32)
    for t in range(nt):
        a,b=grads(kk,kt,va,t*T,T,(kb<=qb) if t<nt//2 else (kb<qb))
        dk=dk+a; dv=dv+b
    nkk,nkt,nva=prep(nk,nv)
    sk=jnp.zeros((C,128),f32); sv=jnp.zeros((C,128),f32)
    for t in range(nt//2,nt):
        a,b=grads(nkk,nkt,nva,t*T,T,kb==qb)
        sk=sk+a; sv=sv+b
    keep=keep_ref[...]
    dk=dk+sk*keep; dv=dv+sv*keep
    dkv_ref[own,0:128]=(dk*SC).astype(bf)
    dkv_ref[own,128:256]=dv.astype(bf)
    def bbody(j,_):
        sl=pl.ds(pl.multiple_of(j*CC,CC),CC)
        kk,kt,va=prep(kv_ref[sl,0:128],kv_ref[sl,128:256])
        dk=dv=None
        for t in range(2048//TT):
            a,b=grads(kk,kt,va,t*TT,TT)
            dk=a if dk is None else dk+a; dv=b if dv is None else dv+b
        dkv_ref[sl,0:128]=(dk*SC).astype(bf)
        dkv_ref[sl,128:256]=dv.astype(bf)
        return 0
    lax.fori_loop(0,nfull,bbody,0)
    def zbody(j,_):
        sl=pl.ds(pl.multiple_of(j*C,C),C)
        dkv_ref[sl,:]=jnp.zeros((C,256),bf)
        return 0
    lax.fori_loop(c+1,32,zbody,0)
    for t in range(nt):
        o_ref[:, 1024+t*128:1024+(t+1)*128]=(dqt[:, t*T:(t+1)*T]*SC).T.astype(bf)


def attend(c, qd, kv, nkv, keep):
    vm = pl.BlockSpec(memory_space=pltpu.VMEM)
    return pl.pallas_call(
        functools.partial(kernel, TT=512, CC=256),
        out_shape=(jax.ShapeDtypeStruct((256, 2048), bf), jax.ShapeDtypeStruct((8192, 256), bf)),
        in_specs=[pl.BlockSpec(memory_space=pltpu.SMEM), vm, vm, vm, vm],
        out_specs=(vm, vm),
        scratch_shapes=[
            pltpu.VMEM((256, 2048), bf),
            pltpu.VMEM((256, 2048), bf),
            pltpu.VMEM((128, 2048), f32),
            pltpu.VMEM((128, 2048), f32),
            pltpu.VMEM((8, 2048), f32),
        ],
        compiler_params=pltpu.CompilerParams(vmem_limit_bytes=48 * 1024 * 1024),
        cost_estimate=pl.CostEstimate(flops=60_000_000_000, bytes_accessed=12_000_000, transcendentals=30_000_000),
        name="attend",
    )(c, qd, kv, nkv, keep)


X_GROUPS = [[x * 8 + z for x in range(4)] for z in range(8)]
Z_GROUPS = [[x * 8 + z for z in range(8)] for x in range(4)]
LEVELS = 8


def to_heads(parts):
    cut = [p.reshape(32, 8, -1) for p in parts]
    sent = jnp.transpose(jnp.concatenate(cut, axis=2), (1, 0, 2))
    got = lax.all_to_all(sent, "head", split_axis=0, concat_axis=0, tiled=True)
    return got.reshape(256, -1)


def to_tokens(rows, parts):
    got = lax.all_to_all(rows.reshape(8, 32, -1), "head", split_axis=0, concat_axis=0, tiled=True)
    got = jnp.transpose(got, (1, 0, 2)).reshape(32, 8, parts, -1)
    return tuple(got[:, :, i].reshape(32, -1) for i in range(parts))


def on_device(q_clean, k_clean, v_clean, q_noised, masked, noise_level, mask_key, mask_value, d_clean, d_noised):
    kv = to_heads((k_clean, v_clean))
    kv_all = lax.all_gather(kv, "ctx", axis=0, tiled=True)
    qd = to_heads((q_clean, q_noised, d_clean, d_noised))
    onehot = (noise_level[:, None] == jnp.arange(LEVELS, dtype=jnp.int32)[None, :]).astype(bf)
    table = jnp.dot(onehot, jnp.concatenate([mask_key, mask_value], axis=1), preferred_element_type=f32).astype(bf)
    table = jnp.repeat(table, BLOCK, axis=0)
    nkv = jnp.where((masked == 1)[:, None], table, kv)
    keep = jnp.broadcast_to((masked == 0).astype(f32)[:, None], (256, 128))
    c = lax.axis_index("ctx").reshape(1)
    rows, dkv = attend(c, qd, kv_all, nkv, keep)
    dkv = lax.psum_scatter(dkv, "ctx", scatter_dimension=0, tiled=True, axis_index_groups=X_GROUPS)
    dkv = lax.psum_scatter(dkv, "ctx", scatter_dimension=0, tiled=True, axis_index_groups=Z_GROUPS)
    return to_tokens(rows, 4) + to_tokens(dkv, 2)


def solution(mesh):
    tokens = P(("ctx", "head"), None)
    return jax.shard_map(
        on_device,
        mesh=mesh,
        in_specs=(tokens,) * 4 + (P("ctx"), P("ctx"), P(None, "head"), P(None, "head"), tokens, tokens),
        out_specs=(tokens,) * 6,
        check_vma=False,
    )
```

time: 800 us -> 327 us (0.41)
  waiting for transfers between devices: 534 us -> 243 us
  loops' own time: 84 us -> 0 us
  local copies, waits for them, and re-layouts: 59.3 us -> 11.6 us
  starting transfers between devices: 53.8 us -> 13.5 us
  matrix products: 20.4 us -> 0.19 us
  Pallas kernels: 0 us -> 11.9 us
  blocking collectives: 19.8 us -> 31.3 us
    reduce_scatter x1 -> x2, waiting for transfers between devices: 409 us -> 170 us  [on_device(): lax.psum_scatter(dkv, 'ctx', scatter_dimension=0, tiled=True, axis_index_...]
    another operation x34 -> x0, loops' own time: 84 us -> none  [the longest x1 42.1 us: fold_clean(): lax.scan(fold_advance, carried, (key_blocks, value_blocks, starts))]
    all_to_all x10 -> x2, starting transfers between devices: 53.7 us -> 13.4 us  [the longest x1 9.05 us: to_tokens(): lax.all_to_all(rows.reshape(8, 32, -1), 'head', split_axis=0, concat_axis...]
    all_gather x2 -> x1, waiting for transfers between devices: 93.6 us -> 58.2 us  [on_device(): kv_all = lax.all_gather(kv, 'ctx', axis=0, tiled=True)]
    dot_general x14 -> x1, matrix products: 20.4 us -> 0.19 us  [on_device(): jnp.dot(onehot, jnp.concatenate([mask_key, mask_value], axis=1), preferre...]
    dynamic_slice x32 -> x0, local copies, waits for them, and re-layouts: 19.7 us -> none  [fold_clean(): lax.scan(fold_advance, carried, (key_blocks, value_blocks, starts))]
    all_to_all x10 -> x2, waiting for transfers between devices: 31 us -> 14.8 us  [the longest x1 14.8 us: to_heads(): got = lax.all_to_all(sent, 'head', split_axis=0, concat_axis=0, tiled=True)]
    all_to_all x16 -> x0, local copies, waits for them, and re-layouts: 15.9 us -> none  [the longest x2 2.48 us: on_device(): lax.all_to_all(out_rows[row_count:], 'head', split_axis=0, concat_axis=1,...]
  transfers between devices with their start and end apart: 13 -> 5, of which waited for: 12 -> 4; matrix products, arithmetic and copies ran while one was open for 4% -> 3% of each run, Pallas kernels for 0% -> 0%
where the time goes in v1:
time: 327 us
  waiting for transfers between devices  243 us (74%)
  blocking collectives  31.3 us (10%)
  between operations  13.9 us (4%)
  starting transfers between devices  13.5 us (4%)
  Pallas kernels  11.9 us (4%)
  local copies, waits for them, and re-layouts  11.6 us (4%)
    reduce_scatter x2, waiting for transfers between devices, on_device(): lax.psum_scatter(dkv, 'ctx', scatter_dimension=0, tiled=True, axis_index_...  170 us
    all_gather x1, waiting for transfers between devices, on_device(): kv_all = lax.all_gather(kv, 'ctx', axis=0, tiled=True)  58.2 us
    all_to_all x1, blocking collectives, to_tokens(): lax.all_to_all(rows.reshape(8, 32, -1), 'head', split_axis=0, concat_axis...  19.8 us
    all_to_all x1, waiting for transfers between devices, to_heads(): got = lax.all_to_all(sent, 'head', split_axis=0, concat_axis=0, tiled=True)  14.8 us
    pallas_call x1, Pallas kernels, attend(): pl.pallas_call(functools.partial(kernel, TT=512, CC=256), out_shape=(jax....  11.9 us
    all_to_all x1, blocking collectives, to_heads(): got = lax.all_to_all(sent, 'head', split_axis=0, concat_axis=0, tiled=True)  11.6 us
    all_to_all x1, starting transfers between devices, to_tokens(): lax.all_to_all(rows.reshape(8, 32, -1), 'head', split_axis=0, concat_axis...  9.05 us
  transfers between devices with their start and end apart: 5, of which 4 were waited for; matrix products, arithmetic and copies ran while one was open for 3% of the time, Pallas kernels for 0%

profile of v1, /device:TPU:1, one launch (start us, length us, event | category | flops | bytes accessed | tf_op | source)
XLA Modules:
  0.0 326.7 jit_solution(3399533704169379152)
XLA Ops:
  7.2 0.0 copy-start
  7.2 0.0 copy-start.2
  7.2 0.0 copy-start.3
  7.2 0.0 all-gather.2.cloned.1.call-start
  7.2 0.8 copy-done
  8.0 0.9 copy_bitcast_fusion.6
  8.9 11.6 %all_to_all.20 = bf16[8,32,256]{2,1,0:T(8,128)(2,1)} all-to-all(bf16[8,32,256]{2,1,0:T(8,128)(2,1)S(1)} %maximum_bitcast_fusion.1), channel_id=1, replica_groups=mesh['ctx'=32,'head'=8] {'head'}, dimensions={0} | all-to-all | bytes 262144 | tf_op jit(solution)/shard_map/all_to_all | solution.py:163
  20.5 0.0 all-gather.2.cloned.1.call-update
  20.5 1.1 copy_bitcast_fusion.2
  21.6 0.0 copy-done.2
  21.6 0.0 copy-done.3
  21.7 0.0 copy-start.4
  21.7 0.0 copy-start.5
  21.7 0.0 copy-start.6
  21.7 0.0 copy-start.7
  21.7 0.0 copy-start.1
  21.7 1.1 maximum_bitcast_fusion
  22.8 4.3 %all-to-all-start = ((bf16[8,32,2048]{2,1,0:T(8,128)(2,1)}), bf16[8,32,2048]{2,1,0:T(8,128)(2,1)S(1)}, u32[]{:S(2)}, u32[]{:S(2)}) async-start(bf16[8,32,2048]{2,1,0:T(8,128)(2,1)} %maximum_bitcast_fusion), calls=%async_computation | async-start | bytes 2097152 | tf_op jit(solution)/shard_map/all_to_all | solution.py:163
  27.2 0.0 reduce-scatter.3.cloned.1.call-start
  27.2 0.0 copy-done.4
  27.2 0.0 copy-done.5
  27.2 0.0 copy-done.6
  27.2 0.0 copy-done.7
  27.2 0.2 convolution_convert_fusion
  27.4 0.0 copy-done.1
  27.4 0.1 bitcast_select_fusion.nkv_ref
  27.5 14.8 %all-to-all-done = bf16[8,32,2048]{2,1,0:T(8,128)(2,1)S(1)} async-done(((bf16[8,32,2048]{2,1,0:T(8,128)(2,1)}), bf16[8,32,2048]{2,1,0:T(8,128)(2,1)S(1)}, u32[]{:S(2)}, u32[]{:S(2)}) %all-to-all-start) | async-done | bytes 1048608 | tf_op jit(solution)/shard_map/all_to_all | solution.py:163
  42.3 58.2 %all-gather.2.cloned.1.call-done.kv_ref = bf16[8192,256]{1,0:T(8,128)(2,1)} async-done(((bf16[256,256]{1,0:T(8,128)(2,1)}), bf16[8192,256]{1,0:T(8,128)(2,1)}) %all-gather.2.cloned.1.call-update) | async-done | bytes 4194320 | tf_op jit(solution)/shard_map/all_gather | solution.py:175
  100.5 0.1 broadcast_in_dim.22.keep_ref
  100.5 11.9 %attend.1 = (bf16[256,2048]{1,0:T(8,128)(2,1)S(1)}, bf16[8192,256]{1,0:T(8,128)(2,1)}) custom-call(s32[1]{0:T(128)} %bitcast.c_ref, bf16[256,2048]{1,0:T(8,128)(2,1)S(1)} %bitcast.68, bf16[8192,256]{1,0:T(8,128)(2,1)} %all-gather.2.cloned.1.call-done.kv_ref, bf16[256,256]{1,0:T(8,128)(2,1)S(1)} %bitcast_select_fusion.nkv_ref, ...), custom_call_target="tpu_custom_call" | custom-call | flops 60000002048 | bytes 12000000 | tf_op jit(solution)/shard_map/attend/pallas_call | solution.py:137
  112.5 0.0 reduce-scatter.3.cloned.1.call-update
  112.5 0.0 reduce-scatter.5.cloned.1.call-start
  112.6 153.6 %reduce-scatter.3.cloned.1.call-done = bf16[2048,256]{1,0:T(8,128)(2,1)} async-done(((bf16[8192,256]{1,0:T(8,128)(2,1)}), bf16[2048,256]{1,0:T(8,128)(2,1)}) %reduce-scatter.3.cloned.1.call-update) | async-done | bytes 1048592 | tf_op jit(solution)/shard_map/reduce_scatter | solution.py:184
  266.1 0.0 reduce-scatter.5.cloned.1.call-update
  266.2 19.8 %all_to_all.21 = bf16[8,32,2048]{2,1,0:T(8,128)(2,1)S(1)} all-to-all(bf16[8,32,2048]{2,1,0:T(8,128)(2,1)S(1)} %bitcast.69), channel_id=1, replica_groups=mesh['ctx'=32,'head'=8] {'head'}, dimensions={0} | all-to-all | bytes 2097152 | tf_op jit(solution)/shard_map/all_to_all | solution.py:168
  285.9 0.8 reshape.68
  286.7 16.4 %reduce-scatter.5.cloned.1.call-done = bf16[256,256]{1,0:T(8,128)(2,1)} async-done(((bf16[2048,256]{1,0:T(8,128)(2,1)}), bf16[256,256]{1,0:T(8,128)(2,1)}) %reduce-scatter.5.cloned.1.call-update) | async-done | bytes 131088 | tf_op jit(solution)/shard_map/reduce_scatter | solution.py:185
  303.1 9.0 %all-to-all-start.3 = ((bf16[8,32,256]{2,1,0:T(8,128)(2,1)}), bf16[8,32,256]{2,1,0:T(8,128)(2,1)S(1)}, u32[]{:S(2)}, u32[]{:S(2)}) async-start(bf16[8,32,256]{2,1,0:T(8,128)(2,1)} %bitcast.87), calls=%async_computation.5 | async-start | bytes 262144 | tf_op jit(solution)/shard_map/all_to_all | solution.py:168
  312.2 2.0 fusion.5
  314.1 0.3 copy.31
  314.4 0.8 copy.43
  315.2 0.3 copy.30
  315.5 0.8 copy.42
  316.3 0.3 copy.29
  316.6 0.8 copy.41
  317.4 0.3 copy.28
  317.6 0.8 copy.40
  318.4 0.0 all-to-all-done.3
  318.5 0.2 fusion.6
  318.7 0.1 copy.33
  318.8 0.6 copy.54
  319.4 0.1 copy.32
  319.5 0.6 copy.55
  (4 shorter events, 0.1 us)
Async XLA Ops:
  7.2 0.8 copy-start
  7.2 14.4 %copy-start.2 = (bf16[32,4096]{1,0:T(8,128)(2,1)S(1)}, bf16[32,4096]{1,0:T(8,128)(2,1)}, u32[]{:S(2)}) copy-start(bf16[32,4096]{1,0:T(8,128)(2,1)} %param.19) | copy-start | bytes 786436
  7.2 14.4 %copy-start.3 = (bf16[32,4096]{1,0:T(8,128)(2,1)S(1)}, bf16[32,4096]{1,0:T(8,128)(2,1)}, u32[]{:S(2)}) copy-start(bf16[32,4096]{1,0:T(8,128)(2,1)} %param.18) | copy-start | bytes 786436
  7.2 93.3 %all-gather.2.cloned.1.call-start = ((), (), s32[]{:S(2)}) async-start(), calls=%async_computation.6 | async-start | bytes 4325376 | tf_op jit(solution)/shard_map/all_gather | solution.py:175
  21.7 5.5 %copy-start.4 = (s32[256]{0:T(256)S(1)}, s32[256]{0:T(256)}, u32[]{:S(2)}) copy-start(s32[256]{0:T(256)} %param.14) | copy-start | bytes 3076
  21.7 5.5 %copy-start.5 = (bf16[8,128]{1,0:T(8,128)(2,1)S(1)}, bf16[8,128]{1,0:T(8,128)(2,1)}, u32[]{:S(2)}) copy-start(bf16[8,128]{1,0:T(8,128)(2,1)} %param.17) | copy-start | bytes 6148
  21.7 5.5 %copy-start.6 = (bf16[8,128]{1,0:T(8,128)(2,1)S(1)}, bf16[8,128]{1,0:T(8,128)(2,1)}, u32[]{:S(2)}) copy-start(bf16[8,128]{1,0:T(8,128)(2,1)} %param.16) | copy-start | bytes 6148
  21.7 5.5 %copy-start.7 = (s32[8]{0:T(128)S(1)}, s32[8]{0:T(128)}, u32[]{:S(2)}) copy-start(s32[8]{0:T(128)} %param.15) | copy-start | bytes 100
  21.7 5.7 %copy-start.1 = (bf16[8,32,256]{2,1,0:T(8,128)(2,1)S(1)}, bf16[8,32,256]{2,1,0:T(8,128)(2,1)}, u32[]{:S(2)}) copy-start(bf16[8,32,256]{2,1,0:T(8,128)(2,1)} %all_to_all.20) | copy-start | bytes 393220
  22.8 19.4 %all-to-all-start = ((bf16[8,32,2048]{2,1,0:T(8,128)(2,1)}), bf16[8,32,2048]{2,1,0:T(8,128)(2,1)S(1)}, u32[]{:S(2)}, u32[]{:S(2)}) async-start(bf16[8,32,2048]{2,1,0:T(8,128)(2,1)} %maximum_bitcast_fusion), calls=%async_computation | async-start | bytes 2097152 | tf_op jit(solution)/shard_map/all_to_all | solution.py:163
  27.2 239.0 %reduce-scatter.3.cloned.1.call-start = ((), (), s32[]{:S(2)}) async-start(), calls=%async_computation.7 | async-start | bytes 5242880 | tf_op jit(solution)/shard_map/reduce_scatter | solution.py:184
  112.5 190.6 %reduce-scatter.5.cloned.1.call-start = ((), (), s32[]{:S(2)}) async-start(), calls=%async_computation.8 | async-start | bytes 1179648 | tf_op jit(solution)/shard_map/reduce_scatter | solution.py:185
  303.1 15.3 %all-to-all-start.3 = ((bf16[8,32,256]{2,1,0:T(8,128)(2,1)}), bf16[8,32,256]{2,1,0:T(8,128)(2,1)S(1)}, u32[]{:S(2)}, u32[]{:S(2)}) async-start(bf16[8,32,256]{2,1,0:T(8,128)(2,1)} %bitcast.87), calls=%async_computation.5 | async-start | bytes 262144 | tf_op jit(solution)/shard_map/all_to_all | solution.py:168
Sparse Core Ops, SparseCore 0:
  20.6 79.7 all-gather.1
  112.6 153.4 reduce-scatter.2
  268.8 34.2 reduce-scatter.4
